TPU v7x, 32 devices: a whole 2x2x4 slice. The times are simulated.
32 devices in a mesh: row: 8 (over z, x), col: 4 (over y, core).
Axes of the slice: x: 2, y: 2, z: 4, core: 2. Of those that a mesh axis runs over, the one named last changes fastest.
Arguments:
- activations: bfloat16 [8, 1024, 8192], P(None, 'col', 'row'), may hold values from -6 to 6
- output_gradients: bfloat16 [8, 1024, 8192], P(None, 'row', 'col'), may hold values from -6 to 6
- second_moment: float32 [8192, 8192], P('col', 'row'), may hold values from 0.0001 to 1, as said below
- proj_out: bfloat16 [256, 8192], P(None, 'col'), may hold values from -0.13258252 to 0.13258252
- proj_in: bfloat16 [256, 8192], P(None, 'row'), may hold values from -0.0625 to 0.0625
- queries: bfloat16 [2048, 65536], P(None, ('row', 'col')), may hold values from -6 to 6
Outputs:
- scores: float32 [8, 2048], replicated
Inputs may be any that keep to these rules, and one draw needn't show every extreme that they name: second_moment is positive.
All inputs are finite; a program needn't handle non-finite values.
Results may differ from a plain program's by a relative error of at most 0.0003.
Values may be sent and summed in bfloat16 or wider, within the bound.
A program may use at most 256 MiB of HBM per device.

v0:
```python
import jax
import jax.numpy as jnp
from jax import lax
from jax.sharding import PartitionSpec as P


def body(activations, output_gradients, second_moment, proj_out, proj_in, queries):
    gathered = lax.all_gather(activations, "col", axis=1, tiled=True)
    examples = gathered.shape[0]
    tile = jnp.einsum(
        "etc,eti->eci",
        lax.all_gather(output_gradients, "row", axis=1, tiled=True),
        gathered,
        preferred_element_type=jnp.float32,
    )
    corrected = tile * lax.rsqrt(second_moment + 1e-08)[None]
    partial_amount = jnp.einsum(
        "kc,eci->eki", proj_out.astype(jnp.float32), corrected, precision=lax.Precision.HIGHEST
    )
    local_proj = jnp.einsum(
        "eki,ji->ekj", partial_amount, proj_in.astype(jnp.float32), precision=lax.Precision.HIGHEST
    )
    flattened_projection = local_proj.reshape(examples, local_proj.shape[1] * local_proj.shape[2])
    rowwise_split = lax.psum_scatter(flattened_projection, "row", scatter_dimension=1, tiled=True)
    projected = lax.psum_scatter(rowwise_split, "col", scatter_dimension=1, tiled=True)
    query_f = queries.astype(jnp.float32)
    square_part = jnp.sum(projected * projected, axis=1)
    square_total = lax.psum(square_part, ("row", "col"))
    unit = projected * lax.rsqrt(square_total + 1e-06)[:, None]
    part_scores = jnp.dot(unit, query_f.T, precision=lax.Precision.HIGHEST)
    scores = lax.psum(part_scores, ("row", "col"))
    return scores


def solution(mesh):
    in_specs = (
        P(None, "col", "row"),
        P(None, "row", "col"),
        P("col", "row"),
        P(None, "col"),
        P(None, "row"),
        P(None, ("row", "col")),
    )
    out_specs = P()
    return jax.shard_map(body, mesh=mesh, in_specs=in_specs, out_specs=out_specs, check_vma=False)
```

profile of v0, /device:TPU:0, one launch (start us, length us, event | category | flops | bytes accessed | tf_op | source)
XLA Modules:
  0.0 1145.8 jit_solution(11496555266475084772)
XLA Ops:
  6.5 0.0 copy-start
  6.5 0.0 all-gather.5.cloned.1.call-start
  6.5 0.7 all-gather.5.cloned.1.call-update
  7.3 0.0 all-gather.3.cloned.1.call-start
  7.3 0.7 all-gather.3.cloned.1.call-update
  8.0 0.0 reduce-scatter.3.cloned.1.call-start
  8.1 8.7 add_rsqrt_fusion
  16.7 100.9 %all-gather.5.cloned.1.call-done = bf16[8,1024,1024]{2,1,0:T(8,128)(2,1)} async-done(((bf16[8,256,1024]{2,1,0:T(8,128)(2,1)}), bf16[8,1024,1024]{2,1,0:T(8,128)(2,1)}) %all-gather.5.cloned.1.call-update) | async-done | bytes 16777232 | tf_op jit(solution)/shard_map/all_gather | solution.py:8
  117.6 639.3 %all-gather.3.cloned.1.call-done = bf16[8,1024,2048]{2,1,0:T(8,128)(2,1)} async-done(((bf16[8,128,2048]{2,1,0:T(8,128)(2,1)}), bf16[8,1024,2048]{2,1,0:T(8,128)(2,1)}) %all-gather.3.cloned.1.call-update) | async-done | bytes 33554448 | tf_op jit(solution)/shard_map/all_gather | solution.py:12
  756.9 49.0 %fusion.13 = f32[8,2048,1024]{2,1,0:T(8,128)} fusion(bf16[8,1024,2048]{2,1,0:T(8,128)(2,1)} %all-gather.3.cloned.1.call-done, bf16[8,1024,1024]{2,1,0:T(8,128)(2,1)} %all-gather.5.cloned.1.call-done), kind=kOutput, calls=%fused_computation.14 | convolution fusion | flops 34359738368 | bytes 117440512 | tf_op jit(solution)/shard_map/etc,eti->eci/dot_general | solution.py:10
  805.9 0.0 copy-done
  805.9 0.0 copy-start.1
  805.9 64.4 %fusion = f32[8,1024,256]{1,2,0:T(8,128)} fusion(f32[8,2048,1024]{2,1,0:T(8,128)} %fusion.13, f32[2048,1024]{1,0:T(8,128)} %add_rsqrt_fusion, bf16[256,2048]{1,0:T(8,128)(2,1)S(1)} %copy-done), kind=kOutput, calls=%fused_computation | convolution fusion | flops 51556384768 | bytes 84934656 | tf_op jit(solution)/shard_map/kc,eci->eki/dot_general | solution.py:17
  870.3 0.0 copy-done.1
  870.3 6.3 fusion.5
  876.6 2.6 copy.7
  879.1 0.0 reduce-scatter.3.cloned.1.call-update
  879.2 0.0 reduce-scatter.5.cloned.1.call-start
  879.2 67.8 %reduce-scatter.3.cloned.1.call-done = f32[8,8192]{1,0:T(8,128)} async-done(((f32[8,65536]{1,0:T(8,128)}), f32[8,8192]{1,0:T(8,128)}) %reduce-scatter.3.cloned.1.call-update) | async-done | bytes 262160 | tf_op jit(solution)/shard_map/reduce_scatter | solution.py:24
  947.0 0.0 reduce-scatter.5.cloned.1.call-update
  947.0 0.0 all-reduce.2.cloned.1.call-start
  947.1 21.3 %reduce-scatter.5.cloned.1.call-done = f32[8,2048]{1,0:T(8,128)} async-done(((f32[8,8192]{1,0:T(8,128)}), f32[8,2048]{1,0:T(8,128)}) %reduce-scatter.5.cloned.1.call-update) | async-done | bytes 65552 | tf_op jit(solution)/shard_map/reduce_scatter | solution.py:25
  968.3 1.0 multiply_reduce_fusion
  969.3 39.4 %psum.14 = f32[8]{0:T(128)S(1)} all-reduce(f32[8]{0:T(128)S(1)} %multiply_reduce_fusion), channel_id=1, replica_groups=mesh['row'=8,'col'=4] {'row','col'}, use_global_device_ids=true, to_apply=%region_3.0 | all-reduce | flops 8 | bytes 64 | tf_op jit(solution)/shard_map/psum | solution.py:28
  1008.7 10.6 fusion.10
  1019.3 0.0 all-reduce.2.cloned.1.call-update
  1019.3 118.4 %all-reduce.2.cloned.1.call-done = f32[8,2048]{1,0:T(8,128)} async-done(((f32[8,2048]{1,0:T(8,128)}), f32[8,2048]{1,0:T(8,128)}) %all-reduce.2.cloned.1.call-update) | async-done | bytes 65552 | tf_op jit(solution)/shard_map/psum | solution.py:31
  1137.7 1.5 copy.9
  (1 shorter events, 0.0 us)
Async XLA Ops:
  6.5 799.4 %copy-start = (bf16[256,2048]{1,0:T(8,128)(2,1)S(1)}, bf16[256,2048]{1,0:T(8,128)(2,1)}, u32[]{:S(2)}) copy-start(bf16[256,2048]{1,0:T(8,128)(2,1)} %param.9) | copy-start | bytes 3145732
  6.5 111.0 %all-gather.5.cloned.1.call-start = ((), (), s32[]{:S(2)}) async-start(), calls=%async_computation.3 | async-start | bytes 20971520 | tf_op jit(solution)/shard_map/all_gather | solution.py:8
  7.3 749.6 %all-gather.3.cloned.1.call-start = ((), (), s32[]{:S(2)}) async-start(), calls=%async_computation.2 | async-start | bytes 37748736 | tf_op jit(solution)/shard_map/all_gather | solution.py:12
  8.0 939.0 %reduce-scatter.3.cloned.1.call-start = ((), (), s32[]{:S(2)}) async-start(), calls=%async_computation.4 | async-start | bytes 2359296 | tf_op jit(solution)/shard_map/reduce_scatter | solution.py:24
  805.9 64.4 %copy-start.1 = (bf16[256,1024]{1,0:T(8,128)(2,1)S(1)}, bf16[256,1024]{1,0:T(8,128)(2,1)}, u32[]{:S(2)}) copy-start(bf16[256,1024]{1,0:T(8,128)(2,1)} %param.10) | copy-start | bytes 1572868
  879.2 89.2 %reduce-scatter.5.cloned.1.call-start = ((), (), s32[]{:S(2)}) async-start(), calls=%async_computation.5 | async-start | bytes 327680 | tf_op jit(solution)/shard_map/reduce_scatter | solution.py:25
  947.0 190.7 %all-reduce.2.cloned.1.call-start = ((), (), s32[]{:S(2)}) async-start(), calls=%async_computation.6 | async-start | bytes 131072 | tf_op jit(solution)/shard_map/psum | solution.py:31
Sparse Core Ops, SparseCore 0:
  8.9 108.6 all-gather.4
  119.1 637.7 all-gather.2
  879.3 67.6 reduce-scatter.2
  949.3 18.9 reduce-scatter.4
  1019.5 118.2 all-reduce.1
where the time goes:
time: 1150 us
  waiting for transfers between devices  949 us (83%)
  matrix products  130 us (11%)
  blocking collectives  39.4 us (3%)
  between operations  13.2 us (1%)
    all_gather x1, waiting for transfers between devices, body(): lax.all_gather(output_gradients, 'row', axis=1, tiled=True)  639 us
    psum x1, waiting for transfers between devices, body(): scores = lax.psum(part_scores, ('row', 'col'))  118 us
    all_gather x1, waiting for transfers between devices, body(): gathered = lax.all_gather(activations, 'col', axis=1, tiled=True)  101 us
    reduce_scatter x1, waiting for transfers between devices, body(): lax.psum_scatter(flattened_projection, 'row', scatter_dimension=1, tiled=...  67.8 us
    dot_general x1, matrix products, body(): jnp.einsum('kc,eci->eki', proj_out.astype(jnp.float32), corrected, precis...  64.4 us
    dot_general x1, matrix products, body(): jnp.einsum('etc,eti->eci', lax.all_gather(output_gradients, 'row', axis=1...  49 us
    psum x1, blocking collectives, body(): square_total = lax.psum(square_part, ('row', 'col'))  39.4 us
  transfers between devices with their start and end apart: 5, of which 5 were waited for; matrix products, arithmetic and copies ran while one was open for 1% of the time, Pallas kernels for 0%

commit v1 on v0

v1 whole, which is shorter than its diff:
```python
import functools

import jax
import jax.numpy as jnp
from jax import lax
from jax.experimental import pallas as pl
from jax.experimental.pallas import tpu as pltpu
from jax.sharding import PartitionSpec as P

MESH = pl.DeviceIdType.MESH
F32 = jnp.float32
BF16 = jnp.bfloat16


def split2(v):
    hi = v.astype(BF16)
    return hi, (v - hi.astype(F32)).astype(BF16)


def kernel(nrow, ncol, nz, act, grad, smom, pout, pin, qry, out, gall, aall,
           gbuf, abuf, scale, qbuf, part, loc, rs, red, sc_src, sc_buf, fin,
           lsem, ldsem, grecv, upsem, dnsem, xsem, arecv, asem,
           rs_send, rs_recv, sc_send, sc_recv, fin_send, fin_recv):
    nx = nrow // nz
    nd = nrow * ncol
    ne, tr, nc = grad.shape
    tc, ni = act.shape[1], act.shape[2]
    ko, ki = pout.shape[0], pin.shape[0]
    own_rows = ko // nd
    pieces = fin.shape[0]
    stride = nd // pieces
    r = lax.axis_index("row")
    c = lax.axis_index("col")
    z, x = r // nx, r % nx
    me = r * ncol + c

    def spot(d):
        return {"row": d // ncol, "col": d % ncol}

    barrier = pltpu.get_barrier_semaphore()

    def greet(k, carry):
        pl.semaphore_signal(barrier, inc=1, device_id=spot((me + k) % nd), device_id_type=MESH)
        return carry

    local = [
        pltpu.make_async_copy(smom, scale, lsem.at[0]),
        pltpu.make_async_copy(qry, qbuf, lsem.at[1]),
        pltpu.make_async_copy(grad, gall.at[:, pl.ds(r * tr, tr), :], lsem.at[2]),
        pltpu.make_async_copy(act, aall.at[:, pl.ds(c * tc, tc), :], lsem.at[3]),
    ]
    lax.fori_loop(1, nd, greet, 0)
    for copy in local:
        copy.start()
    pl.semaphore_wait(barrier, nd - 1)

    def block(e, row):
        return gall.at[e, pl.ds(row * tr, tr), :]

    def g_copy(e, zs, send_sem, target, own=False):
        row = zs * nx + x
        return pltpu.make_async_remote_copy(
            src_ref=grad.at[e] if own else block(e, row),
            dst_ref=block(e, row),
            send_sem=send_sem,
            recv_sem=grecv.at[e, row],
            device_id={"row": target},
            device_id_type=MESH,
        )

    def up(e, zs, own=False):
        return g_copy(e, zs, upsem.at[e, zs], (z + 1) * nx + x, own)

    def down(e, zs, own=False):
        return g_copy(e, zs, dnsem.at[e, zs], (z - 1) * nx + x, own)

    def across(e, zs, k, own=False):
        return g_copy(e, zs, xsem.at[e, zs, k], z * nx + (x + k) % nx, own)

    def a_copy(e, k):
        rows = pl.ds(c * tc, tc)
        return pltpu.make_async_remote_copy(
            src_ref=act.at[e],
            dst_ref=aall.at[e, rows, :],
            send_sem=asem.at[e, k],
            recv_sem=arecv.at[e, c],
            device_id={"col": (c + k) % ncol},
            device_id_type=MESH,
        )

    def g_arrived(e, row):
        pltpu.make_async_copy(block(e, row), block(e, row), grecv.at[e, row]).wait()

    def own_sends(e):
        @pl.when(z < nz - 1)
        def _():
            up(e, z, True).start()

        @pl.when(z > 0)
        def _():
            down(e, z, True).start()

        for k in range(1, nx):
            across(e, z, k, True).start()
        for k in range(1, ncol):
            a_copy(e, k).start()

    def forward(e, d):
        @pl.when(z - d >= 0)
        def _():
            zs = z - d
            g_arrived(e, zs * nx + x)

            @pl.when(z < nz - 1)
            def _():
                up(e, zs).start()

            for k in range(1, nx):
                across(e, zs, k).start()

        @pl.when(z + d < nz)
        def _():
            zs = z + d
            g_arrived(e, zs * nx + x)

            @pl.when(z > 0)
            def _():
                down(e, zs).start()

            for k in range(1, nx):
                across(e, zs, k).start()

    def loads(e):
        return (
            pltpu.make_async_copy(gall.at[e], gbuf, ldsem.at[0]),
            pltpu.make_async_copy(aall.at[e], abuf, ldsem.at[1]),
        )

    def load(e):
        for k in range(1, nx):
            for zs in range(nz):
                g_arrived(e, zs * nx + (x + k) % nx)
        for k in range(1, ncol):
            rows = pl.ds(((c + k) % ncol) * tc, tc)
            whole = aall.at[e, rows, :]
            pltpu.make_async_copy(whole, whole, arecv.at[e, (c + k) % ncol]).wait()
        for copy in loads(e):
            copy.start()

    def rs_block(d):
        return pl.ds(pl.multiple_of((d * own_rows) // 8 * 8, 8), 8)

    width = min(512, nc)

    def compute(e):
        for copy in loads(e):
            copy.wait()
        part[...] = jnp.zeros_like(part)

        def columns(j, carry):
            cols = pl.ds(pl.multiple_of(j * width, width), width)
            tile = lax.dot_general(
                gbuf[:, cols], abuf[...], (((0,), (0,)), ((), ())), preferred_element_type=F32
            )
            hi, lo = split2(tile * scale[cols, :])
            po = pout[:, cols]
            part[...] += jnp.dot(po, hi, preferred_element_type=F32) + jnp.dot(
                po, lo, preferred_element_type=F32
            )
            return carry

        lax.fori_loop(0, nc // width, columns, 0)
        hi, lo = split2(part[...])
        nt = (((1,), (1,)), ((), ()))
        loc[e] = lax.dot_general(hi, pin[...], nt, preferred_element_type=F32) + lax.dot_general(
            lo, pin[...], nt, preferred_element_type=F32
        )
        rs[me, e] = loc[e, rs_block(me), :]

        def send(k, carry):
            d = (me + k) % nd
            pltpu.make_async_remote_copy(
                src_ref=loc.at[e, rs_block(d), :],
                dst_ref=rs.at[me, e],
                send_sem=rs_send,
                recv_sem=rs_recv,
                device_id=spot(d),
                device_id_type=MESH,
            ).start()
            return carry

        lax.fori_loop(1, nd, send, 0)

    own_sends(0)
    own_sends(1)
    local[0].wait()
    lines = min(256, nc)

    def invert(j, carry):
        rows = pl.ds(pl.multiple_of(j * lines, lines), lines)
        scale[rows, :] = lax.rsqrt(scale[rows, :] + 1e-08)
        return carry

    lax.fori_loop(0, nc // lines, invert, 0)
    for copy in local[1:]:
        copy.wait()

    def step(s, carry):
        @pl.when(s + 2 < ne)
        def _():
            own_sends(s + 2)

        for d in range(1, nz):
            @pl.when((s - d + 1 >= 0) & (s - d + 1 < ne))
            def _():
                forward(s - d + 1, d)

        @pl.when(s - nz >= 0)
        def _():
            compute(s - nz)

        @pl.when((s - nz + 1 >= 0) & (s - nz + 1 < ne))
        def _():
            load(s - nz + 1)

        return carry

    lax.fori_loop(0, ne + nz, step, 0)

    def sent(e, carry):
        for k in range(1, ncol):
            a_copy(e, k).wait_send()
        for zs in range(nz):
            for k in range(1, nx):
                across(e, zs, k).wait_send()

            @pl.when((zs <= z) & (z < nz - 1))
            def _():
                up(e, zs).wait_send()

            @pl.when((zs >= z) & (z > 0))
            def _():
                down(e, zs).wait_send()

        return carry

    landed = rs.at[pl.ds(0, nd - 1)]
    pltpu.make_async_copy(landed, landed, rs_recv).wait()
    red[...] = lax.fori_loop(1, nd, lambda k, v: v + rs[k], rs[0])
    first = (me * own_rows) % 8 if own_rows < 8 else 0
    squares = jnp.zeros((ne, ki), F32)
    total = jnp.zeros((3 * ne, qbuf.shape[0]), F32)
    for k in range(own_rows):
        row = red[:, first + k, :]
        squares += row * row
        hi = row.astype(BF16).astype(F32)
        mid = (row - hi).astype(BF16).astype(F32)
        lhs = jnp.concatenate([hi, mid, row - hi - mid], axis=0).astype(BF16)
        total += lax.dot_general(
            lhs, qbuf[:, k * ki:(k + 1) * ki], (((1,), (1,)), ((), ())), preferred_element_type=F32
        )
    scores = total[:ne] + total[ne:2 * ne] + total[2 * ne:]
    sq = jnp.broadcast_to(jnp.sum(squares, axis=1, keepdims=True), (ne, 128))
    for p in range(pieces):
        sc_src[p, 0] = scores[:, p * 128:(p + 1) * 128]
        sc_src[p, 1] = sq

    mine = me // stride
    reducer = me % stride == 0

    def to_reducer(p, carry):
        @pl.when(p * stride != me)
        def _():
            pltpu.make_async_remote_copy(
                src_ref=sc_src.at[p],
                dst_ref=sc_buf.at[me],
                send_sem=sc_send,
                recv_sem=sc_recv,
                device_id=spot(p * stride),
                device_id_type=MESH,
            ).start()

        return carry

    lax.fori_loop(0, pieces, to_reducer, 0)

    @pl.when(reducer)
    def _():
        sc_buf[me] = sc_src[mine]
        whole = sc_buf.at[pl.ds(0, nd - 1)]
        pltpu.make_async_copy(whole, whole, sc_recv).wait()
        both = lax.fori_loop(1, nd, lambda k, v: v + sc_buf[k], sc_buf[0])
        fin[mine] = both[0] * lax.rsqrt(both[1] + 1e-06)

        def to_all(k, carry):
            pltpu.make_async_remote_copy(
                src_ref=fin.at[mine],
                dst_ref=fin.at[mine],
                send_sem=fin_send,
                recv_sem=fin_recv,
                device_id=spot((me + k) % nd),
                device_id_type=MESH,
            ).start()
            return carry

        lax.fori_loop(1, nd, to_all, 0)

    lax.fori_loop(0, ne, sent, 0)
    pltpu.make_async_copy(landed, landed, rs_send).wait()

    def finish(count):
        src = sc_src.at[pl.ds(0, count)]
        pltpu.make_async_copy(src, src, sc_send).wait()
        got = fin.at[pl.ds(0, count)]
        pltpu.make_async_copy(got, got, fin_recv).wait()

    @pl.when(reducer)
    def _():
        finish(pieces - 1)
        gone = sc_buf.at[pl.ds(0, nd - 1), 0]
        pltpu.make_async_copy(gone, gone, fin_send).wait()

    @pl.when(jnp.logical_not(reducer))
    def _():
        finish(pieces)

    for p in range(pieces):
        out[:, p * 128:(p + 1) * 128] = fin[p]


def body(nrow, ncol, activations, output_gradients, second_moment, proj_out, proj_in, queries):
    ne, tc, ni = activations.shape
    tr, nc = output_gradients.shape[1:]
    ko, ki = proj_out.shape[0], proj_in.shape[0]
    nq, nf = queries.shape
    nz = 4 if nrow % 4 == 0 else 1
    nd = nrow * ncol
    pieces = nq // 128
    while nd % pieces:
        pieces //= 2
    seq = tr * nrow
    dma = pltpu.SemaphoreType.DMA
    hbm = pl.BlockSpec(memory_space=pl.ANY)
    vmem = pl.BlockSpec(memory_space=pltpu.VMEM)
    return pl.pallas_call(
        functools.partial(kernel, nrow, ncol, nz),
        out_shape=(
            jax.ShapeDtypeStruct((ne, nq), F32),
            jax.ShapeDtypeStruct((ne, seq, nc), BF16),
            jax.ShapeDtypeStruct((ne, seq, ni), BF16),
        ),
        in_specs=[hbm, hbm, hbm, vmem, vmem, hbm],
        out_specs=(vmem, hbm, hbm),
        scratch_shapes=[
            pltpu.VMEM((seq, nc), BF16),
            pltpu.VMEM((seq, ni), BF16),
            pltpu.VMEM((nc, ni), F32),
            pltpu.VMEM((nq, nf), BF16),
            pltpu.VMEM((ko, ni), F32),
            pltpu.VMEM((ne, ko, ki), F32),
            pltpu.VMEM((nd, ne, 8, ki), F32),
            pltpu.VMEM((ne, 8, ki), F32),
            pltpu.VMEM((pieces, 2, ne, 128), F32),
            pltpu.VMEM((nd, 2, ne, 128), F32),
            pltpu.VMEM((pieces, ne, 128), F32),
            dma((4,)),
            dma((2,)),
            dma((ne, nrow)),
            dma((ne, nz)),
            dma((ne, nz)),
            dma((ne, nz, nrow // nz)),
            dma((ne, ncol)),
            dma((ne, ncol)),
            dma, dma, dma, dma, dma, dma,
        ],
        compiler_params=pltpu.CompilerParams(
            collective_id=0, has_side_effects=True, vmem_limit_bytes=58 * 2**20
        ),
    )(activations, output_gradients, second_moment, proj_out, proj_in, queries)[0]


def solution(mesh):
    in_specs = (
        P(None, "col", "row"),
        P(None, "row", "col"),
        P("col", "row"),
        P(None, "col"),
        P(None, "row"),
        P(None, ("row", "col")),
    )
    run = functools.partial(body, mesh.shape["row"], mesh.shape["col"])
    return jax.shard_map(run, mesh=mesh, in_specs=in_specs, out_specs=P(), check_vma=False)
```

time: 1150 us -> 652 us (0.57)
  waiting for transfers between devices: 949 us -> 0 us
  Pallas kernels: 0 us -> 651 us
  matrix products: 130 us -> 0 us
  blocking collectives: 39.4 us -> 0 us
  between operations: 13.2 us -> 0.01 us
    all_gather x2 -> x0, waiting for transfers between devices: 740 us -> none  [the longest x1 639 us: body(): lax.all_gather(output_gradients, 'row', axis=1, tiled=True)]
    pallas_call x0 -> x1, Pallas kernels: none -> 651 us  [body(): pl.pallas_call(functools.partial(kernel, nrow, ncol, nz), out_shape=(jax....]
    dot_general x4 -> x0, matrix products: 130 us -> none  [the longest x1 64.4 us: body(): jnp.einsum('kc,eci->eki', proj_out.astype(jnp.float32), corrected, precis...]
    psum x1 -> x0, waiting for transfers between devices: 118 us -> none  [body(): scores = lax.psum(part_scores, ('row', 'col'))]
    reduce_scatter x2 -> x0, waiting for transfers between devices: 89.1 us -> none  [the longest x1 67.8 us: body(): lax.psum_scatter(flattened_projection, 'row', scatter_dimension=1, tiled=...]
    psum x1 -> x0, blocking collectives: 39.4 us -> none  [body(): square_total = lax.psum(square_part, ('row', 'col'))]
  transfers between devices with their start and end apart: 5 -> 0, of which waited for: 5 -> 0; matrix products, arithmetic and copies ran while one was open for 1% -> 0% of each run, Pallas kernels for 0% -> 0%
where the time goes in v1:
time: 652 us
  Pallas kernels  651 us (100%)
    pallas_call x1, Pallas kernels, body(): pl.pallas_call(functools.partial(kernel, nrow, ncol, nz), out_shape=(jax....  651 us

profile of v1, /device:TPU:0, one launch (start us, length us, event | category | flops | bytes accessed | tf_op | source)
XLA Modules:
  0.0 652.2 jit_solution(12733674483558329440)
XLA Ops:
  0.0 650.7 %shard_map.64 = (f32[8,2048]{1,0:T(8,128)}, bf16[8,1024,2048]{2,1,0:T(8,128)(2,1)}, bf16[8,1024,1024]{2,1,0:T(8,128)(2,1)}) custom-call(bf16[8,256,1024]{2,1,0:T(8,128)(2,1)} %act.1, bf16[8,128,2048]{2,1,0:T(8,128)(2,1)} %grad.1, f32[2048,1024]{1,0:T(8,128)} %smom.1, bf16[256,2048]{1,0:T(8,128)(2,1)} %pout.1, bf16[256,1024]{1,0:T(8,128)(2,1)} %pin.1, ...), custom_call_target="tpu_custom_call" | custom-call | tf_op jit(solution)/shard_map/pallas_call | solution.py:345
  650.7 1.5 copy.8

commit v2 on v1

--- a/solution.py
+++ b/solution.py
@@ -46,8 +46,6 @@
     local = [
         pltpu.make_async_copy(smom, scale, lsem.at[0]),
         pltpu.make_async_copy(qry, qbuf, lsem.at[1]),
-        pltpu.make_async_copy(grad, gall.at[:, pl.ds(r * tr, tr), :], lsem.at[2]),
-        pltpu.make_async_copy(act, aall.at[:, pl.ds(c * tc, tc), :], lsem.at[3]),
     ]
     lax.fori_loop(1, nd, greet, 0)
     for copy in local:
@@ -131,10 +129,16 @@
                 across(e, zs, k).start()
 
     def loads(e):
-        return (
-            pltpu.make_async_copy(gall.at[e], gbuf, ldsem.at[0]),
-            pltpu.make_async_copy(aall.at[e], abuf, ldsem.at[1]),
-        )
+        copies = []
+        for k in range(nrow):
+            rows = pl.ds(((r + k) % nrow) * tr, tr)
+            src = gall.at[e, rows, :] if k else grad.at[e]
+            copies.append(pltpu.make_async_copy(src, gbuf.at[rows, :], ldsem.at[k]))
+        for k in range(ncol):
+            rows = pl.ds(((c + k) % ncol) * tc, tc)
+            src = aall.at[e, rows, :] if k else act.at[e]
+            copies.append(pltpu.make_async_copy(src, abuf.at[rows, :], ldsem.at[nrow + k]))
+        return copies
 
     def load(e):
         for k in range(1, nx):
@@ -202,8 +206,7 @@
         return carry
 
     lax.fori_loop(0, nc // lines, invert, 0)
-    for copy in local[1:]:
-        copy.wait()
+    local[1].wait()
 
     def step(s, carry):
         @pl.when(s + 2 < ne)
@@ -363,8 +366,8 @@
             pltpu.VMEM((pieces, 2, ne, 128), F32),
             pltpu.VMEM((nd, 2, ne, 128), F32),
             pltpu.VMEM((pieces, ne, 128), F32),
-            dma((4,)),
             dma((2,)),
+            dma((nrow + ncol,)),
             dma((ne, nrow)),
             dma((ne, nz)),
             dma((ne, nz)),

time: 652 us -> 421 us (0.65)
  Pallas kernels: 651 us -> 420 us
    pallas_call x1, Pallas kernels: 651 us -> 420 us  [body(): pl.pallas_call(functools.partial(kernel, nrow, ncol, nz), out_shape=(jax....]
where the time goes in v2:
time: 421 us
  Pallas kernels  420 us (100%)
    pallas_call x1, Pallas kernels, body(): pl.pallas_call(functools.partial(kernel, nrow, ncol, nz), out_shape=(jax....  420 us

profile of v2, /device:TPU:0, one launch (start us, length us, event | category | flops | bytes accessed | tf_op | source)
XLA Modules:
  0.0 421.3 jit_solution(9302921159899840609)
XLA Ops:
  0.0 419.8 %shard_map.64 = (f32[8,2048]{1,0:T(8,128)}, bf16[8,1024,2048]{2,1,0:T(8,128)(2,1)}, bf16[8,1024,1024]{2,1,0:T(8,128)(2,1)}) custom-call(bf16[8,256,1024]{2,1,0:T(8,128)(2,1)} %act.1, bf16[8,128,2048]{2,1,0:T(8,128)(2,1)} %grad.1, f32[2048,1024]{1,0:T(8,128)} %smom.1, bf16[256,2048]{1,0:T(8,128)(2,1)} %pout.1, bf16[256,1024]{1,0:T(8,128)(2,1)} %pin.1, ...), custom_call_target="tpu_custom_call" | custom-call | tf_op jit(solution)/shard_map/pallas_call | solution.py:348
  419.8 1.5 copy.8
